TPU v7x, 256 devices: a whole 4x4x8 slice. The times are simulated.
256 devices in a mesh: item: 128 (over y, z_hi, x, core), batch: 2 (over z_lo).
Axes of the slice: x: 4, y: 4, z: 8 (z_hi: 4, z_lo: 2; z = z_hi * 2 + z_lo), core: 2. Of those that a mesh axis runs over, the one named last changes fastest.
Arguments:
- user_vectors: bfloat16 [32768, 256], P(('item', 'batch')), may hold values from -70 to 70
- item_table: float32 [262144, 256], P('item'), may hold values from -0.3 to 0.3
- grad_accum: float32 [262144, 256], P('item'), may hold values from 0.05 to 0.5
- log_prob: float32 [262144], P('item'), may hold values from -16 to -6
- positive_shard: int32 [32768, 1], P(('item', 'batch')), may hold values from 0 to 127; in each aligned block of 128 rows (0 to 127, 128 to 255, ...) at most 2 rows name the same one
- positive_row: int32 [32768], P(('item', 'batch')), may hold values from 0 to 2047
- negatives: int32 [65536], P('item'), may hold values from 0 to 2047
Outputs:
- new_table: float32 [262144, 256], P('item')
- new_accum: float32 [262144, 256], P('item')
- user_loss: float32 [32768], P(('item', 'batch'))
Inputs may be any that keep to these rules, and one draw needn't show every extreme that they name: `positive_shard`: in the 128 user rows of one device at most 2 name one shard, and exactly 2 do for some shard.
All inputs are finite; a program needn't handle non-finite values.
Results may differ from a plain program's by a relative error of at most 0.0046.
Values may be sent and summed in bfloat16 or wider, within the bound.
A program may use at most 192 MiB of HBM per device.

v0:
```python
import jax
import jax.numpy as jnp
from jax import lax
from jax.sharding import PartitionSpec as P

LOGIT_SCALE = 2.5
STEP_RATE = 0.05
NEG_FLOOR = -1e30


def merged_2(value, axis, combine):
    everything = jax.tree.map(lambda part: lax.all_gather(part, axis), value)
    first = jax.tree.map(lambda part: part[0], everything)

    def step(k, so_far):
        return combine(so_far, jax.tree.map(lambda part: part[k], everything))

    return lax.fori_loop(1, lax.axis_size(axis), step, first)


def combine_stats(earlier, later):
    peak_score = jnp.maximum(earlier[0], later[0])
    merged = earlier[1] * jnp.exp(earlier[0] - peak_score) + later[1] * jnp.exp(
        later[0] - peak_score
    )
    return (peak_score, merged)


def per_device(
    user_vectors, item_table, grad_accum, log_prob, positive_shard, positive_row, negatives
):
    n_item = lax.axis_size("item")
    my_index = lax.axis_index("item")
    rows_dev = user_vectors.shape[0]
    slots_each = max(2, 2 * rows_dev // n_item)
    n_slots = n_item * slots_each
    group_rows = rows_dev * n_item
    neg_rows = item_table[negatives].astype(jnp.bfloat16)
    neg_bias = log_prob[negatives]

    def score_block(user_block):
        product = lax.dot_general(
            user_block, neg_rows, (((1,), (1,)), ((), ())), preferred_element_type=jnp.float32
        )
        return LOGIT_SCALE * product - neg_bias[None, :]

    owner_shard = positive_shard[:, 0]
    owner_hot = (owner_shard[:, None] == jnp.arange(n_item, dtype=jnp.int32)[None, :]).astype(
        jnp.int32
    )
    slot_rank = jnp.sum((jnp.cumsum(owner_hot, axis=0) - owner_hot) * owner_hot, axis=1)
    target = owner_shard * slots_each + slot_rank
    placement = (target[:, None] == jnp.arange(n_slots, dtype=jnp.int32)[None, :]).astype(
        jnp.float32
    )

    def to_slots(values):
        return lax.dot_general(
            placement, values, (((0,), (0,)), ((), ())), precision=lax.Precision.HIGHEST
        )

    def from_slots(values):
        return jnp.dot(placement, values, precision=lax.Precision.HIGHEST)

    users_wide = user_vectors.astype(jnp.float32)
    request = (to_slots((positive_row + 1).astype(jnp.float32)) - 1.0).astype(jnp.int32)
    asked = lax.all_to_all(request, "item", split_axis=0, concat_axis=0, tiled=True)
    row_index = jnp.maximum(asked, 0)
    live_mask = (asked >= 0).astype(jnp.float32)
    reply_rows = item_table[row_index] * live_mask[:, None]
    reply_bias = log_prob[row_index] * live_mask
    got_rows, got_bias = (
        lax.all_to_all(reply_rows, "item", split_axis=0, concat_axis=0, tiled=True),
        lax.all_to_all(reply_bias, "item", split_axis=0, concat_axis=0, tiled=True),
    )
    pos_vec = from_slots(got_rows).astype(jnp.bfloat16).astype(jnp.float32)
    pos_score = LOGIT_SCALE * jnp.sum(users_wide * pos_vec, axis=1) - from_slots(got_bias)
    init_max = jnp.full((group_rows,), NEG_FLOOR, jnp.float32)
    init_sum = jnp.zeros((group_rows,), jnp.float32)
    own_start = my_index * rows_dev
    previous = (init_max, init_sum)
    score_tile = score_block(lax.all_gather(user_vectors, "item", axis=0, tiled=True))
    tile_max = jnp.max(score_tile, axis=1)
    tile_sum = jnp.sum(jnp.exp(score_tile - tile_max[:, None]), axis=1)
    updated = combine_stats(previous, (tile_max, tile_sum))
    part_max = updated[0]
    part_sum = updated[1]
    own_stats = (
        lax.dynamic_slice_in_dim(part_max, own_start, rows_dev),
        lax.dynamic_slice_in_dim(part_sum, own_start, rows_dev),
    )
    own_stats = combine_stats(own_stats, (pos_score, jnp.ones_like(pos_score)))
    part_max = lax.dynamic_update_slice_in_dim(part_max, own_stats[0], own_start, 0)
    part_sum = lax.dynamic_update_slice_in_dim(part_sum, own_stats[1], own_start, 0)
    total_max, total_sum = merged_2((part_max, part_sum), "item", combine_stats)
    log_norm = total_max + jnp.log(total_sum)
    own_norm = lax.dynamic_slice_in_dim(log_norm, own_start, rows_dev)
    user_loss = own_norm - pos_score
    coefficient = jnp.exp(pos_score - own_norm) - 1.0
    shard_rows = lax.all_gather(user_vectors, "item", axis=0, tiled=True)
    probs = jnp.exp(score_block(shard_rows) - log_norm[:, None]).astype(jnp.bfloat16)
    neg_sum = lax.dot_general(
        probs, shard_rows, (((0,), (0,)), ((), ())), preferred_element_type=jnp.float32
    )
    grad_slots = to_slots((LOGIT_SCALE * coefficient)[:, None] * users_wide)
    pos_terms = lax.all_to_all(grad_slots, "item", split_axis=0, concat_axis=0, tiled=True)
    grad = jnp.zeros_like(item_table).at[negatives].add(LOGIT_SCALE * neg_sum)
    grad = grad.at[row_index].add(pos_terms)
    grand_grad = lax.psum(grad, "batch")
    new_accum = grad_accum + grand_grad * grand_grad
    new_table = item_table - STEP_RATE * grand_grad * lax.rsqrt(new_accum)
    return (new_table, new_accum, user_loss)


def solution(mesh):
    in_specs = (
        P(("item", "batch"), None),
        P("item", None),
        P("item", None),
        P("item"),
        P(("item", "batch"), None),
        P(("item", "batch")),
        P("item"),
    )
    out_specs = (P("item", None), P("item", None), P(("item", "batch")))
    return jax.shard_map(
        per_device, mesh=mesh, in_specs=in_specs, out_specs=out_specs, check_vma=False
    )
```

profile of v0, /device:TPU:1, one launch (start us, length us, event | category | flops | bytes accessed | tf_op | source)
XLA Modules:
  0.0 636.9 jit_solution(16473847459243973203)
XLA Ops:
  11.4 28.1 %all_to_all.39 = s32[128,2,1]{1,2,0:T(1,128)S(1)} all-to-all(s32[128,2,1]{1,2,0:T(1,128)S(1)} %bitcast.63), channel_id=1, replica_groups=mesh['item'=128,'batch'=2] {'item'}, dimensions={0} | all-to-all | bytes 2048 | tf_op jit(solution)/shard_map/all_to_all | solution.py:67
  39.7 1.7 gather_fusion.3
  42.2 5.8 all-to-all-start.2
  48.1 2.6 gather_fusion.2
  51.7 8.3 %all-to-all-done.2 = f32[128,2,1]{1,2,0:T(1,128)S(1)} async-done(((f32[128,2,1]{1,2,0:T(1,128)}), f32[128,2,1]{1,2,0:T(1,128)S(1)}, u32[]{:S(2)}, u32[]{:S(2)}) %all-to-all-start.2) | async-done | bytes 1056 | tf_op jit(solution)/shard_map/all_to_all | solution.py:74
  60.0 5.9 all-to-all-start.1
  67.1 3.1 gather_fusion.1
  70.3 1.6 gather_fusion
  73.3 7.9 %all-to-all-done.1 = f32[128,2,256]{2,1,0:T(2,128)S(1)} async-done(((f32[128,2,256]{2,1,0:T(2,128)}), f32[128,2,256]{2,1,0:T(2,128)S(1)}, u32[]{:S(2)}, u32[]{:S(2)}) %all-to-all-start.1) | async-done | bytes 262176 | tf_op jit(solution)/shard_map/all_to_all | solution.py:73
  81.8 24.1 %all-gather.6.cloned.1.call-done = bf16[16384,256]{1,0:T(8,128)(2,1)} async-done(((bf16[128,256]{1,0:T(8,128)(2,1)}), bf16[16384,256]{1,0:T(8,128)(2,1)}) %all-gather.6.cloned.1.call-update) | async-done | bytes 8388624 | tf_op jit(solution)/shard_map/all_gather | solution.py:100
  105.9 16.6 %fusion.27 = (f32[16384]{0:T(1024)S(1)}, f32[512,16384]{1,0:T(8,128)}) fusion(f32[512]{0:T(512)S(1)} %gather_fusion.1, bf16[512,256]{1,0:T(8,128)(2,1)S(1)} %gather_fusion, bf16[16384,256]{1,0:T(8,128)(2,1)} %all-gather.6.cloned.1.call-done), kind=kOutput, calls=%fused_computation.69 | convolution fusion | flops 4320116736 | bytes 42272768 | tf_op jit(solution)/shard_map/dot_general | solution.py:42
  122.4 13.1 %exponential_reduce_fusion = f32[16384]{0:T(1024)S(1)} fusion(f32[512,16384]{1,0:T(8,128)} %get-tuple-element.163, f32[16384]{0:T(1024)S(1)} %get-tuple-element.162), kind=kLoop, calls=%fused_computation.10 | loop fusion | flops 16760832 | bytes 33685504 | tf_op jit(solution)/shard_map/reduce_sum | solution.py:84
  137.5 88.2 %all-gather.8.cloned.1.call-done = f32[128,1,16384]{2,1,0:T(1,128)} async-done(((f32[1,1,16384]{2,1,0:T(1,128)}), f32[128,1,16384]{2,1,0:T(1,128)}) %all-gather.8.cloned.1.call-update) | async-done | bytes 8388624 | tf_op jit(solution)/shard_map/all_gather | solution.py:12
  225.6 13.1 %copy.23 = f32[128,1,16384]{2,0,1:T(8,128)} copy(f32[128,1,16384]{2,1,0:T(1,128)} %all-gather.8.cloned.1.call-done) | data formatting | bytes 16777216
  238.8 79.8 %all-gather.10.cloned.1.call-done = f32[128,1,16384]{2,1,0:T(1,128)} async-done(((f32[1,1,16384]{2,1,0:T(1,128)}), f32[128,1,16384]{2,1,0:T(1,128)}) %all-gather.10.cloned.1.call-update) | async-done | bytes 8388624 | tf_op jit(solution)/shard_map/all_gather | solution.py:12
  318.5 13.4 %copy.22 = f32[128,1,16384]{2,0,1:T(8,128)} copy(f32[128,1,16384]{2,1,0:T(1,128)} %all-gather.10.cloned.1.call-done) | data formatting | bytes 16777216
  332.0 176.6 %while.17 = (s32[]{:T(128)}, f32[16384]{0:T(1024)S(1)}, f32[16384]{0:T(1024)S(1)}, f32[128,16384]{1,0:T(8,128)}, f32[128,16384]{1,0:T(8,128)}, /*index=5*/s32[]{:T(128)}, s32[]{:T(128)}, s32[]{:T(128)}) while((s32[]{:T(128)}, f32[16384]{0:T(1024)S(1)}, f32[16384]{0:T(1024)S(1)}, f32[128,16384]{1,0:T(8,128)}, f32[128,16384]{1,0:T(8,128)}, ...), condition=%wide.region_6.7_spmd, body=%wide.region_5.6_spmd.sunk | while | flops 98309 | bytes 655483 | solution.py:18
  333.3 1.3 constant_dynamic-slice_fusion.3
  510.4 10.2 %all-to-all-start.3 = ((f32[128,2,256]{2,1,0:T(2,128)}), f32[128,2,256]{2,1,0:T(2,128)S(1)}, u32[]{:S(2)}, u32[]{:S(2)}) async-start(f32[128,2,256]{2,1,0:T(2,128)} %all_to_all.32), calls=%async_computation.3 | async-start | bytes 524288 | tf_op jit(solution)/shard_map/all_to_all | solution.py:106
  520.6 18.4 %fusion.2 = f32[512,256]{1,0:T(8,128)} fusion(bf16[16384,256]{1,0:T(8,128)(2,1)} %all-gather.6.cloned.1.call-done, f32[512,16384]{1,0:T(8,128)} %get-tuple-element.163, f32[16384]{0:T(1024)S(1)} %log_add_fusion), kind=kOutput, calls=%fused_computation.18 | convolution fusion | flops 4311875584 | bytes 42532864 | tf_op jit(solution)/shard_map/dot_general | solution.py:102
  539.0 5.2 scatter_custom_fusion
  544.4 4.7 scatter_fusion
  549.1 76.1 %all-reduce.2.cloned.1.call-done = f32[2048,256]{1,0:T(8,128)} async-done(((f32[2048,256]{1,0:T(8,128)}), f32[2048,256]{1,0:T(8,128)}) %all-reduce.2.cloned.1.call-update) | async-done | bytes 2097168 | tf_op jit(solution)/shard_map/psum | solution.py:109
  625.2 4.8 multiply_subtract_fusion.1
  (308 shorter events, 185.7 us)
Async XLA Ops:
  7.2 32.5 %copy-start = (f32[2048]{0:T(1024)S(1)}, f32[2048]{0:T(1024)}, u32[]{:S(2)}) copy-start(f32[2048]{0:T(1024)} %param.12) | copy-start | bytes 24580
  7.2 74.2 %copy-start.3 = (bf16[128,256]{1,0:T(8,128)(2,1)S(1)}, bf16[128,256]{1,0:T(8,128)(2,1)}, u32[]{:S(2)}) copy-start(bf16[128,256]{1,0:T(8,128)(2,1)} %param.9) | copy-start | bytes 196612
  7.2 63.1 %copy-start.2 = (f32[2048,256]{1,0:T(8,128)S(1)}, f32[2048,256]{1,0:T(8,128)}, u32[]{:S(2)}) copy-start(f32[2048,256]{1,0:T(8,128)} %param.10) | copy-start | bytes 6291460
  7.2 98.6 %all-gather.6.cloned.1.call-start = ((), (), s32[]{:S(2)}) async-start(), calls=%async_computation.4 | async-start | bytes 8454144 | tf_op jit(solution)/shard_map/all_gather | solution.py:100
  42.2 17.8 %all-to-all-start.2 = ((f32[128,2,1]{1,2,0:T(1,128)}), f32[128,2,1]{1,2,0:T(1,128)S(1)}, u32[]{:S(2)}, u32[]{:S(2)}) async-start(f32[128,2,1]{1,2,0:T(1,128)} %bitcast.13), calls=%async_computation.2 | async-start | bytes 131072 | tf_op jit(solution)/shard_map/all_to_all | solution.py:74
  60.0 21.2 %all-to-all-start.1 = ((f32[128,2,256]{2,1,0:T(2,128)}), f32[128,2,256]{2,1,0:T(2,128)S(1)}, u32[]{:S(2)}, u32[]{:S(2)}) async-start(f32[128,2,256]{2,1,0:T(2,128)} %broadcast_multiply_fusion), calls=%async_computation.1 | async-start | bytes 524288 | tf_op jit(solution)/shard_map/all_to_all | solution.py:73
  65.9 159.7 %all-gather.8.cloned.1.call-start = ((), (), s32[]{:S(2)}) async-start(), calls=%async_computation.6 | async-start | bytes 8454144 | tf_op jit(solution)/shard_map/all_gather | solution.py:12
  136.0 0.6 copy-start.5
  136.1 0.9 copy-start.4
  136.7 181.8 %all-gather.10.cloned.1.call-start = ((), (), s32[]{:S(2)}) async-start(), calls=%async_computation.7 | async-start | bytes 8454144 | tf_op jit(solution)/shard_map/all_gather | solution.py:12
  318.5 13.4 %slice-start = ((f32[128,1,16384]{2,1,0:T(1,128)}), f32[1,1,16384]{2,1,0:T(1,128)S(1)}, s32[]{:S(2)}) async-start(f32[128,1,16384]{2,1,0:T(1,128)} %all-gather.8.cloned.1.call-done), calls=%async_computation.8 | async-start | bytes 131072 | tf_op jit(solution)/shard_map/slice | solution.py:13
  318.5 13.4 %slice-start.1 = ((f32[128,1,16384]{2,1,0:T(1,128)}), f32[1,1,16384]{2,1,0:T(1,128)S(1)}, s32[]{:S(2)}) async-start(f32[128,1,16384]{2,1,0:T(1,128)} %all-gather.10.cloned.1.call-done), calls=%async_computation.9 | async-start | bytes 131072 | tf_op jit(solution)/shard_map/slice | solution.py:13
  510.4 33.8 %all-to-all-start.3 = ((f32[128,2,256]{2,1,0:T(2,128)}), f32[128,2,256]{2,1,0:T(2,128)S(1)}, u32[]{:S(2)}, u32[]{:S(2)}) async-start(f32[128,2,256]{2,1,0:T(2,128)} %all_to_all.32), calls=%async_computation.3 | async-start | bytes 524288 | tf_op jit(solution)/shard_map/all_to_all | solution.py:106
  520.6 104.7 %all-reduce.2.cloned.1.call-start = ((), (), s32[]{:S(2)}) async-start(), calls=%async_computation.5 | async-start | bytes 4194304 | tf_op jit(solution)/shard_map/psum | solution.py:109
  544.2 85.9 %copy-start.1 = (f32[2048]{0:T(1024)S(1)}, f32[2048]{0:T(1024)}, u32[]{:S(2)}) copy-start(f32[2048]{0:T(1024)} %param.12) | copy-start | bytes 24580
Sparse Core Ops, SparseCore 0:
  11.5 94.3 all-gather.5
  136.8 88.7 all-gather.7
  229.6 88.8 all-gather.9
  549.2 75.9 all-reduce.1
where the time goes:
time: 646 us; the launch traced here: 637 us
  waiting for transfers between devices  286 us (44%)
  local copies, waits for them, and re-layouts  203 us (31%)
  other arithmetic  43.1 us (7%)
  matrix products  36.8 us (6%)
  blocking collectives  28.1 us (4%)
  starting transfers between devices  22.7 us (4%)
  between operations  14.3 us (2%)
    all_gather x2, waiting for transfers between devices, merged_2(): everything = jax.tree.map(lambda part: lax.all_gather(part, axis), value)  168 us
    dynamic_slice x127, local copies, waits for them, and re-layouts, step(): return combine(so_far, jax.tree.map(lambda part: part[k], everything))  165 us
    psum x1, waiting for transfers between devices, per_device(): grand_grad = lax.psum(grad, 'batch')  76.1 us
    all_to_all x1, blocking collectives, per_device(): lax.all_to_all(request, 'item', split_axis=0, concat_axis=0, tiled=True)  28.1 us
    unnamed x14, local copies, waits for them, and re-layouts  27.2 us
    all_gather x1, waiting for transfers between devices, per_device(): shard_rows = lax.all_gather(user_vectors, 'item', axis=0, tiled=True)  24.1 us
    dot_general x1, matrix products, per_device(): lax.dot_general(probs, shard_rows, (((0,), (0,)), ((), ())), preferred_el...  18.4 us
    dot_general x1, matrix products, score_block(): lax.dot_general(user_block, neg_rows, (((1,), (1,)), ((), ())), preferred...  16.6 us
  transfers between devices with their start and end apart: 7, of which 6 were waited for; matrix products, arithmetic and copies ran while one was open for 8% of the time, Pallas kernels for 0%

commit v1 on v0

v1 whole, which is shorter than its diff:
```python
import math

import jax
import jax.numpy as jnp
from jax import lax
from jax.experimental import pallas as pl
from jax.experimental.pallas import tpu as pltpu
from jax.sharding import PartitionSpec as P

LOGIT_SCALE = 2.5
STEP_RATE = 0.05
LOG2E = math.log2(math.e)
LN2 = math.log(2.0)
FLOOR = -1e30

BLOCKS = 128
ROWS = 128
WIDTH = 256
ITEMS = 2048
NEGS = 512
STEPS = 64
SLOTS = 256


def order4(q):
    return jnp.where(q < 2, q, 5 - q)


def head_kernel(
    u_ref, ids_ref, negr_ref, lp_ref, table_ref,
    gsum_ref, up_out, r_out, c_out, loss_ref,
    users, scores, negs, bias, tab, tabb, ids_all, first_i, last_i, first_r, last_r,
    slot_i, slot_r, slot_t, slot_lp, slot_pos, slot_u, slot_c,
    stat_out, stat_in, norm_all, acc, gsend, grecv, upx, rx, cx,
    block_sem, send_sem, tab_sem, ids_sem, ids_send, stat_sem, stat_send, norm_sem, norm_send,
    pair_send, pair_recv,
):
    me = lax.axis_index("item")
    group = lax.axis_index("batch")
    other = 1 - group
    core = lax.rem(me, 2)
    sib = me + 1 - 2 * core
    x_pos = lax.rem(me // 2, 4)
    z_pos = lax.rem(me // 8, 4)
    y_pos = me // 32
    outer = jnp.where(core == 0, y_pos, x_pos)
    inner = jnp.where(core == 0, x_pos, y_pos)
    s_out = jnp.where(core == 0, 32, 2)
    s_in = 34 - s_out

    def place(do, di, dz):
        return (
            lax.rem(outer + do, 4) * s_out + lax.rem(inner + di, 4) * s_in
            + lax.rem(z_pos + dz, 4) * 8 + core
        )

    def sib_place(do, di, dz):
        return (
            lax.rem(inner + do, 4) * s_in + lax.rem(outer + di, 4) * s_out
            + lax.rem(z_pos + dz, 4) * 8 + 1 - core
        )

    def parts(t):
        late = jnp.maximum(t - 16, 0)
        k = jnp.where(t < 16, t, jnp.where(t < 48, late // 2, t - 48))
        do = jnp.where(t < 16, 0, jnp.where(t < 48, 1 + 2 * lax.rem(late, 2), 2))
        return do, k // 4, lax.rem(k, 4), k

    def block_copy(b, dev):
        return pltpu.make_async_remote_copy(
            src_ref=users.at[b], dst_ref=users.at[b], send_sem=send_sem,
            recv_sem=block_sem.at[b], device_id={"item": dev},
            device_id_type=pl.DeviceIdType.MESH,
        )

    def forward(t):
        do, ki, kz, k = parts(t)
        di, dz = order4(ki), order4(kz)
        b = place(do, di, dz)

        @pl.when(t > 0)
        def _():
            block_copy(b, sib).wait_recv()

        @pl.when(do == 0)
        def _():
            block_copy(b, place(1, 0, 0)).start()
            block_copy(b, place(3, 0, 0)).start()

            @pl.when(di == 0)
            def _():
                block_copy(b, place(0, 1, 0)).start()
                block_copy(b, place(0, 3, 0)).start()

                @pl.when(dz == 0)
                def _():
                    block_copy(b, place(0, 0, 1)).start()
                    block_copy(b, place(0, 0, 3)).start()

                @pl.when(dz == 1 + 2 * core)
                def _():
                    block_copy(b, place(0, 0, 3 - 2 * core)).start()

            @pl.when((di == 1) & (lax.rem(kz, 2) == 0))
            def _():
                block_copy(b, place(0, 3, 0)).start()

            @pl.when((di == 3) & (lax.rem(kz, 2) == 1))
            def _():
                block_copy(b, place(0, 1, 0)).start()

        @pl.when((do == 1) & (lax.rem(k, 2) == 0))
        def _():
            block_copy(b, place(3, 0, 0)).start()

        @pl.when((do == 3) & (lax.rem(k, 2) == 1))
        def _():
            block_copy(b, place(1, 0, 0)).start()

        block_copy(b, sib).start()

    def blocks_of(t):
        do, ki, kz, _ = parts(t)
        di, dz = order4(ki), order4(kz)
        return place(do, di, dz), sib_place(do, di, dz)

    def peer_copy(src, dst, send, recv, dev):
        return pltpu.make_async_remote_copy(
            src_ref=src, dst_ref=dst, send_sem=send, recv_sem=recv,
            device_id={"item": dev}, device_id_type=pl.DeviceIdType.MESH,
        )

    def wait_bytes(ref, sem):
        pltpu.make_async_copy(ref, ref, sem).wait()

    table_copy = pltpu.make_async_copy(table_ref, tab, tab_sem)
    table_copy.start()
    users[me] = u_ref[...]
    ids_all[me] = ids_ref[...]
    forward(jnp.int32(0))

    @pl.loop(1, BLOCKS)
    def _(j):
        dev = lax.rem(me + j, BLOCKS)
        peer_copy(ids_all.at[me], ids_all.at[me], ids_send, ids_sem, dev).start()

    @pl.loop(1, 4)
    def _(t):
        forward(t)

    table_copy.wait()
    tabb[...] = tab[...].astype(jnp.bfloat16)
    lp2 = lp_ref[...] * LOG2E

    def hot_of(row_cols):
        lane = lax.broadcasted_iota(jnp.int32, row_cols.shape, 1)
        return [row_cols == lane + 128 * j for j in range(ITEMS // 128)]

    def gather(row_cols):
        hots = hot_of(row_cols)
        hot = jnp.concatenate([h.astype(jnp.float32).astype(jnp.bfloat16) for h in hots], axis=1)
        rows = jnp.dot(hot, tabb[...], preferred_element_type=jnp.float32)
        total = jnp.zeros(row_cols.shape, jnp.float32)
        for j, h in enumerate(hots):
            total = total + jnp.where(h, lp2[:, 128 * j : 128 * (j + 1)], 0.0)
        lp_rows = jnp.broadcast_to(jnp.sum(total, axis=1, keepdims=True), row_cols.shape)
        return rows, lp_rows

    neg_cols = jnp.transpose(jnp.broadcast_to(negr_ref[...], (128, NEGS)))
    for q in range(NEGS // 128):
        part = slice(128 * q, 128 * (q + 1))
        rows, lp_rows = gather(neg_cols[part])
        negs[part, :] = rows.astype(jnp.bfloat16)
        bias[part, :] = lp_rows

    @pl.loop(4, 16)
    def _(t):
        forward(t)

    wait_bytes(ids_all.at[pl.ds(0, BLOCKS - 1)], ids_sem)
    ids = ids_all[:, 0, :]
    lane = lax.broadcasted_iota(jnp.int32, (BLOCKS, ROWS), 1)
    mine = (ids // ITEMS) == me
    row = lax.rem(ids, ITEMS)
    wide = (BLOCKS, ROWS)
    lo = jnp.broadcast_to(
        jnp.min(jnp.where(mine, lane, ROWS), axis=1, keepdims=True), wide
    )
    hi = jnp.broadcast_to(jnp.max(jnp.where(mine, lane, -1), axis=1, keepdims=True), wide)
    first_i[...] = jnp.where(lo < ROWS, lo, -1)
    last_i[...] = jnp.where(hi > lo, hi, -1)
    first_r[...] = jnp.broadcast_to(
        jnp.max(jnp.where(mine & (lane == lo), row, -1), axis=1, keepdims=True), wide
    )
    last_r[...] = jnp.broadcast_to(
        jnp.max(jnp.where(mine & (lane == hi) & (hi > lo), row, -1), axis=1, keepdims=True), wide
    )
    sub = lax.broadcasted_iota(jnp.int32, (8, 128), 0)

    @pl.loop(0, STEPS // 2)
    def _(i):
        ivals, rvals = [], []
        for u in range(2):
            for b in blocks_of(2 * i + u):
                ivals += [first_i[pl.ds(b, 1), :], last_i[pl.ds(b, 1), :]]
                rvals += [first_r[pl.ds(b, 1), :], last_r[pl.ds(b, 1), :]]
        islab = jnp.broadcast_to(ivals[0], (8, 128))
        rslab = jnp.broadcast_to(rvals[0], (8, 128))
        for c in range(1, 8):
            islab = jnp.where(sub == c, ivals[c], islab)
            rslab = jnp.where(sub == c, rvals[c], rslab)
        slot_i[pl.ds(8 * i, 8), :] = islab
        slot_r[pl.ds(8 * i, 8), :] = rslab

    for q in range(SLOTS // 128):
        part = slice(128 * q, 128 * (q + 1))
        rows, lp_rows = gather(slot_r[part, :])
        slot_t[part, :] = rows
        slot_lp[part, :] = lp_rows

    lane8 = lax.broadcasted_iota(jnp.int32, (8, 128), 1)

    def slot_masks(i, u):
        islab = slot_i[pl.ds(8 * i, 8), :]
        hit = islab == lane8
        left = hit & (sub >= 4 * u) & (sub < 4 * u + 2)
        right = hit & (sub >= 4 * u + 2) & (sub < 4 * u + 4)
        return jnp.concatenate(
            [jnp.where(left, 1.0, 0.0), jnp.where(right, 1.0, 0.0)], axis=1
        )

    def two_blocks(t):
        b1, b2 = blocks_of(t)
        return jnp.concatenate([users[b1], users[b2]], axis=0)

    def send_stats(b, lse, pos):
        stat_out[b] = jnp.concatenate([lse, pos], axis=0)

        @pl.when(b != me)
        def _():
            peer_copy(stat_out.at[b], stat_in.at[me], stat_send, stat_sem, b).start()

        @pl.when(b == me)
        def _():
            stat_in[b] = stat_out[b]

    @pl.loop(0, STEPS // 2)
    def _(i):
        phase = lax.rem(i, 4)

        @pl.when(phase < 3)
        def _():
            pair = 8 + 3 * (i // 4) + phase
            forward(2 * pair)
            forward(2 * pair + 1)

        gathered = jnp.zeros((8, WIDTH), jnp.float32)
        masks = []
        for u in range(2):
            t = 2 * i + u
            b1, b2 = blocks_of(t)
            block_copy(b2, sib).wait_recv()
            pair_users = jnp.concatenate([users[b1], users[b2]], axis=0)
            mask = slot_masks(i, u)
            masks.append(mask)
            hot = jnp.concatenate([mask, jnp.zeros_like(mask)], axis=0).astype(jnp.bfloat16)
            gathered = gathered + jnp.dot(
                hot, pair_users, preferred_element_type=jnp.float32
            )[0:8]
            raw = lax.dot_general(
                negs[...], pair_users, (((1,), (1,)), ((), ())),
                preferred_element_type=jnp.float32,
            )
            cols = jnp.concatenate([bias[...], bias[...]], axis=1)
            scaled = raw * (LOGIT_SCALE * LOG2E) - cols
            scores[t] = scaled
        slot_u[pl.ds(8 * i, 8), :] = gathered
        dots = jnp.sum(gathered * slot_t[pl.ds(8 * i, 8), :], axis=1, keepdims=True)
        pos = dots * (LOGIT_SCALE * LOG2E) - slot_lp[pl.ds(8 * i, 8), :]
        slot_pos[pl.ds(8 * i, 8), :] = pos
        pos_wide = jnp.concatenate([pos, pos], axis=1)
        for u in range(2):
            t = 2 * i + u
            b1, b2 = blocks_of(t)
            peak = jnp.max(scores[t], axis=0, keepdims=True)
            total = jnp.sum(jnp.exp2(scores[t] - peak), axis=0, keepdims=True)
            lse = peak + jnp.log(total) * LOG2E
            pos_row = jnp.max(
                jnp.where(masks[u] > 0.0, pos_wide, FLOOR), axis=0, keepdims=True
            )
            send_stats(b1, lse[:, :ROWS], pos_row[:, :ROWS])
            send_stats(b2, lse[:, ROWS:], pos_row[:, ROWS:])

    def pair_copy(src, dst, k):
        return pltpu.make_async_remote_copy(
            src_ref=src, dst_ref=dst, send_sem=pair_send.at[k], recv_sem=pair_recv.at[k],
            device_id={"batch": other}, device_id_type=pl.DeviceIdType.MESH,
        )

    upx[group] = slot_u[...].astype(jnp.bfloat16)
    rx[group] = jnp.transpose(slot_r[...])[0:8, :]
    up_copy = pair_copy(upx.at[group], upx.at[group], 0)
    r_copy = pair_copy(rx.at[group], rx.at[group], 1)
    up_copy.start()
    r_copy.start()

    wait_bytes(stat_in.at[pl.ds(0, BLOCKS - 1)], stat_sem)
    lses = stat_in[:, 0, :]
    pos_own = jnp.max(stat_in[:, 1, :], axis=0, keepdims=True)
    top = jnp.maximum(jnp.max(lses, axis=0, keepdims=True), pos_own)
    total = jnp.sum(jnp.exp2(lses - top), axis=0, keepdims=True) + jnp.exp2(pos_own - top)
    norm = top + jnp.log(total) * LOG2E
    norm_all[me] = norm

    @pl.loop(1, BLOCKS)
    def _(j):
        dev = lax.rem(me + j, BLOCKS)
        peer_copy(norm_all.at[me], norm_all.at[me], norm_send, norm_sem, dev).start()

    loss_ref[...] = (norm - pos_own) * LN2
    wait_bytes(norm_all.at[pl.ds(0, BLOCKS - 1)], norm_sem)

    def norm_row(t):
        b1, b2 = blocks_of(t)
        return jnp.concatenate([norm_all[b1], norm_all[b2]], axis=1)

    @pl.loop(0, STEPS // 2)
    def _(i):
        found = jnp.zeros((8, WIDTH), jnp.float32)
        for u in range(2):
            found = found + jnp.where(slot_masks(i, u) > 0.0, norm_row(2 * i + u), 0.0)
        slot_norm = jnp.sum(found, axis=1, keepdims=True)
        live = slot_i[pl.ds(8 * i, 8), :] >= 0
        coefficient = jnp.exp2(slot_pos[pl.ds(8 * i, 8), :] - slot_norm) - 1.0
        slot_c[pl.ds(8 * i, 8), :] = jnp.where(live, LOGIT_SCALE * coefficient, 0.0)

    cx[group] = jnp.transpose(slot_c[...])[0:8, :]
    c_copy = pair_copy(cx.at[group], cx.at[group], 2)
    c_copy.start()

    copies = [up_copy, r_copy, c_copy]
    half = NEGS // 2
    for h in range(2):
        part = slice(half * h, half * (h + 1))
        acc[...] = jnp.zeros_like(acc)

        @pl.loop(0, STEPS // 4)
        def _(g):
            probs, rows = [], []
            for u in range(4):
                t = 4 * g + u
                probs.append(
                    jnp.exp2(scores[t, part, :] - norm_row(t)).astype(jnp.bfloat16)
                )
                rows.append(two_blocks(t))
            acc[...] += jnp.dot(
                jnp.concatenate(probs, axis=1), jnp.concatenate(rows, axis=0),
                preferred_element_type=jnp.float32,
            )

        gsend[h] = acc[...].astype(gsend.dtype)
        g_copy = pair_copy(gsend.at[h], grecv.at[h], 3 + h)
        g_copy.start()
        copies.append(g_copy)

    for copy in copies:
        copy.wait()
    for h in range(2):
        part = slice(half * h, half * (h + 1))
        gsum_ref[part, :] = gsend[h].astype(jnp.float32) + grecv[h].astype(jnp.float32)
    for k in range(2):
        up_out[SLOTS * k : SLOTS * (k + 1), :] = upx[k]
        r_out[:, SLOTS * k : SLOTS * (k + 1)] = rx[k]
        c_out[:, SLOTS * k : SLOTS * (k + 1)] = cx[k]
    wait_bytes(users.at[pl.ds(0, BLOCKS - 1)], send_sem)
    wait_bytes(ids_all.at[pl.ds(0, BLOCKS - 1)], ids_send)
    wait_bytes(stat_in.at[pl.ds(0, BLOCKS - 1)], stat_send)
    wait_bytes(norm_all.at[pl.ds(0, BLOCKS - 1)], norm_send)


def head(u, ids, negr, lp, table):
    f32, bf16, i32 = jnp.float32, jnp.bfloat16, jnp.int32
    vmem = pl.BlockSpec(memory_space=pltpu.VMEM)
    dma = pltpu.SemaphoreType.DMA
    V = pltpu.VMEM
    return pl.pallas_call(
        head_kernel,
        out_shape=(
            jax.ShapeDtypeStruct((NEGS, WIDTH), f32),
            jax.ShapeDtypeStruct((2 * SLOTS, WIDTH), bf16),
            jax.ShapeDtypeStruct((8, 2 * SLOTS), i32),
            jax.ShapeDtypeStruct((8, 2 * SLOTS), f32),
            jax.ShapeDtypeStruct((1, ROWS), f32),
        ),
        in_specs=[vmem, vmem, vmem, vmem, pl.BlockSpec(memory_space=pl.ANY)],
        out_specs=(vmem,) * 5,
        scratch_shapes=[
            V((BLOCKS, ROWS, WIDTH), bf16),
            V((STEPS, NEGS, 2 * ROWS), f32),
            V((NEGS, WIDTH), bf16),
            V((NEGS, 128), f32),
            V((ITEMS, WIDTH), f32),
            V((ITEMS, WIDTH), bf16),
            V((BLOCKS, 1, ROWS), i32),
            V((BLOCKS, ROWS), i32),
            V((BLOCKS, ROWS), i32),
            V((BLOCKS, ROWS), i32),
            V((BLOCKS, ROWS), i32),
            V((SLOTS, 128), i32),
            V((SLOTS, 128), i32),
            V((SLOTS, WIDTH), f32),
            V((SLOTS, 128), f32),
            V((SLOTS, 128), f32),
            V((SLOTS, WIDTH), f32),
            V((SLOTS, 128), f32),
            V((BLOCKS, 2, ROWS), f32),
            V((BLOCKS, 2, ROWS), f32),
            V((BLOCKS, 1, ROWS), f32),
            V((NEGS // 2, WIDTH), f32),
            V((2, NEGS // 2, WIDTH), bf16),
            V((2, NEGS // 2, WIDTH), bf16),
            V((2, SLOTS, WIDTH), bf16),
            V((2, 8, SLOTS), i32),
            V((2, 8, SLOTS), f32),
            dma((BLOCKS,)),
            dma, dma, dma, dma, dma, dma, dma, dma,
            dma((5,)),
            dma((5,)),
        ],
        compiler_params=pltpu.CompilerParams(
            has_side_effects=True, vmem_limit_bytes=58 * 1024 * 1024
        ),
        cost_estimate=pl.CostEstimate(
            flops=3 * 2 * 16384 * NEGS * WIDTH, bytes_accessed=4 << 20,
            transcendentals=2 * 16384 * NEGS,
        ),
        name="sampled_head",
    )(u, ids, negr, lp, table)


TILE = 256


def update_kernel(
    negr_ref, r_ref, c_ref, gsum_ref, up_ref, table_ref, accum_ref,
    new_table_ref, new_accum_ref, g_hi, g_lo,
):
    @pl.when(pl.program_id(0) == 0)
    def _():
        g = LOGIT_SCALE * gsum_ref[...]
        top = g.astype(jnp.bfloat16)
        g_hi[...] = top
        g_lo[...] = (g - top.astype(jnp.float32)).astype(jnp.bfloat16)

    row = lax.broadcasted_iota(jnp.int32, (TILE, NEGS), 0) + TILE * pl.program_id(0)
    hot = jnp.where(row == negr_ref[...], 1.0, 0.0).astype(jnp.bfloat16)
    weight = jnp.where(row == r_ref[0:1, :], c_ref[0:1, :], 0.0)
    w_hi = weight.astype(jnp.bfloat16)
    w_lo = (weight - w_hi.astype(jnp.float32)).astype(jnp.bfloat16)

    def mm(a, b):
        return jnp.dot(a, b, preferred_element_type=jnp.float32)

    grad = (mm(hot, g_hi[...]) + mm(hot, g_lo[...])) + (
        mm(w_hi, up_ref[...]) + mm(w_lo, up_ref[...])
    )
    accum = accum_ref[...] + grad * grad
    new_accum_ref[...] = accum
    new_table_ref[...] = table_ref[...] - STEP_RATE * grad * lax.rsqrt(accum)


def update(negr, rows, coefs, gsum, ups, table, accum):
    whole = lambda shape: pl.BlockSpec(shape, lambda i: (0, 0))
    tile = pl.BlockSpec((TILE, WIDTH), lambda i: (i, 0))
    return pl.pallas_call(
        update_kernel,
        grid=(ITEMS // TILE,),
        out_shape=(jax.ShapeDtypeStruct((ITEMS, WIDTH), jnp.float32),) * 2,
        in_specs=[
            whole((1, NEGS)), whole((8, 2 * SLOTS)), whole((8, 2 * SLOTS)),
            whole((NEGS, WIDTH)), whole((2 * SLOTS, WIDTH)), tile, tile,
        ],
        out_specs=(tile, tile),
        scratch_shapes=[pltpu.VMEM((NEGS, WIDTH), jnp.bfloat16)] * 2,
        compiler_params=pltpu.CompilerParams(vmem_limit_bytes=16 * 1024 * 1024),
        name="table_update",
    )(negr, rows, coefs, gsum, ups, table, accum)


def per_device(
    user_vectors, item_table, grad_accum, log_prob, positive_shard, positive_row, negatives
):
    ids = positive_shard.reshape(1, ROWS) * ITEMS + positive_row.reshape(1, ROWS)
    negr = negatives.reshape(1, NEGS)
    gsum, ups, rows, coefs, loss = head(
        user_vectors, ids, negr, log_prob.reshape(1, ITEMS), item_table
    )
    new_table, new_accum = update(negr, rows, coefs, gsum, ups, item_table, grad_accum)
    return (new_table, new_accum, loss.reshape(ROWS))


def solution(mesh):
    in_specs = (
        P(("item", "batch"), None),
        P("item", None),
        P("item", None),
        P("item"),
        P(("item", "batch"), None),
        P(("item", "batch")),
        P("item"),
    )
    out_specs = (P("item", None), P("item", None), P(("item", "batch")))
    return jax.shard_map(
        per_device, mesh=mesh, in_specs=in_specs, out_specs=out_specs, check_vma=False
    )
```

time: 646 us -> 122 us (0.19); the launches traced: 637 us -> 121 us
  waiting for transfers between devices: 286 us -> 0 us
  local copies, waits for them, and re-layouts: 203 us -> 3.94 us
  Pallas kernels: 0 us -> 115 us
  other arithmetic: 43.1 us -> 1.19 us
  matrix products: 36.8 us -> 0 us
  blocking collectives: 28.1 us -> 0 us
  starting transfers between devices: 22.7 us -> 0 us
  between operations: 14.3 us -> 0.68 us
    all_gather x3 -> x0, waiting for transfers between devices: 192 us -> none  [the longest x2 168 us: merged_2(): everything = jax.tree.map(lambda part: lax.all_gather(part, axis), value)]
    dynamic_slice x127 -> x0, local copies, waits for them, and re-layouts: 165 us -> none  [step(): return combine(so_far, jax.tree.map(lambda part: part[k], everything))]
    pallas_call x0 -> x2, Pallas kernels: none -> 115 us  [the longest x1 110 us: head(): pl.pallas_call(head_kernel, out_shape=(jax.ShapeDtypeStruct((NEGS, WIDTH)...]
    psum x1 -> x0, waiting for transfers between devices: 76.1 us -> none  [per_device(): grand_grad = lax.psum(grad, 'batch')]
    dot_general x6 -> x0, matrix products: 36.8 us -> none  [the longest x1 18.4 us: per_device(): lax.dot_general(probs, shard_rows, (((0,), (0,)), ((), ())), preferred_el...]
    all_to_all x1 -> x0, blocking collectives: 28.1 us -> none  [per_device(): lax.all_to_all(request, 'item', split_axis=0, concat_axis=0, tiled=True)]
    unnamed x14 -> x17, local copies, waits for them, and re-layouts: 27.2 us -> 3.94 us
    all_to_all x3 -> x0, starting transfers between devices: 21.9 us -> none  [the longest x1 10.2 us: per_device(): lax.all_to_all(grad_slots, 'item', split_axis=0, concat_axis=0, tiled=True)]
  transfers between devices with their start and end apart: 7 -> 0, of which waited for: 6 -> 0; matrix products, arithmetic and copies ran while one was open for 8% -> 0% of each run, Pallas kernels for 0% -> 0%
where the time goes in v1:
time: 122 us; the launch traced here: 121 us
  Pallas kernels  115 us (94%)
  local copies, waits for them, and re-layouts  3.94 us (3%)
    pallas_call x1, Pallas kernels, head(): pl.pallas_call(head_kernel, out_shape=(jax.ShapeDtypeStruct((NEGS, WIDTH)...  110 us
    pallas_call x1, Pallas kernels, update(): pl.pallas_call(update_kernel, grid=(ITEMS // TILE,), out_shape=(jax.Shape...  5.56 us
    unnamed x17, local copies, waits for them, and re-layouts  3.94 us

profile of v1, /device:TPU:1, one launch (start us, length us, event | category | flops | bytes accessed | tf_op | source)
XLA Modules:
  0.0 120.9 jit_solution(8787491730600156880)
XLA Ops:
  0.6 1.2 fusion.ids_ref
  1.8 0.0 copy-start
  1.8 0.0 copy-start.1
  1.8 0.0 copy-start.6
  1.8 109.6 %sampled_head.1 = (f32[512,256]{1,0:T(8,128)}, bf16[512,256]{1,0:T(8,128)(2,1)}, s32[8,512]{1,0:T(8,128)}, f32[8,512]{1,0:T(8,128)}, f32[1,128]{1,0:T(1,128)}) custom-call(bf16[128,256]{1,0:T(8,128)(2,1)} %u_ref.1, s32[1,128]{1,0:T(1,128)} %fusion.ids_ref, s32[1,512]{1,0:T(1,128)} %bitcast.9, f32[1,2048]{1,0:T(1,128)} %bitcast.11, f32[2048,256]{1,0:T(8,128)} %table_ref.3), custom_call_target="tpu_custom_call" | custom-call | flops 12884901888 | bytes 4194304 | tf_op jit(solution)/shard_map/sampled_head/pallas_call | solution.py:386
  111.4 0.0 copy-done
  111.4 0.0 copy-done.1
  111.4 0.0 copy-done.6
  111.4 0.0 copy-start.2
  111.4 1.0 copy-done.2
  112.5 0.0 copy-start.3
  112.5 0.9 copy-done.3
  113.4 0.0 copy-start.4
  113.4 0.7 copy-done.4
  114.1 0.0 copy-start.5
  114.1 0.7 copy-done.5
  114.9 0.0 copy-start.7
  114.9 5.6 %table_update.1 = (f32[2048,256]{1,0:T(8,128)}, f32[2048,256]{1,0:T(8,128)}) custom-call(s32[1,512]{1,0:T(1,128)S(1)} %bitcast.10, s32[8,512]{1,0:T(8,128)S(1)} %copy-done.4, f32[8,512]{1,0:T(8,128)S(1)} %copy-done.5, f32[512,256]{1,0:T(8,128)S(1)} %copy-done.2, bf16[512,256]{1,0:T(8,128)(2,1)S(1)} %copy-done.3, f32[2048,256]{1,0:T(8,128)S(1)} %copy-done, ...), custom_call_target="tpu_custom_call" | custom-call | tf_op jit(solution)/shard_map/table_update/pallas_call | solution.py:475
  120.4 0.0 copy-done.7
  120.4 0.5 copy.11
Async XLA Ops:
  1.8 109.6 %copy-start = (f32[2048,256]{1,0:T(8,128)S(1)}, f32[2048,256]{1,0:T(8,128)}, u32[]{:S(2)}) copy-start(f32[2048,256]{1,0:T(8,128)} %table_ref.3) | copy-start | bytes 6291460
  1.8 109.6 %copy-start.1 = (f32[2048,256]{1,0:T(8,128)S(1)}, f32[2048,256]{1,0:T(8,128)}, u32[]{:S(2)}) copy-start(f32[2048,256]{1,0:T(8,128)} %accum_ref.1) | copy-start | bytes 6291460
  1.8 109.6 %copy-start.6 = (s32[512]{0:T(512)S(1)}, s32[512]{0:T(512)}, u32[]{:S(2)}) copy-start(s32[512]{0:T(512)} %param.13) | copy-start | bytes 6148
  111.4 1.0 copy-start.2
  112.5 0.9 copy-start.3
  113.4 0.7 copy-start.4
  114.1 0.7 copy-start.5
  114.9 5.6 %copy-start.7 = (f32[1,128]{1,0:T(1,128)S(1)}, f32[1,128]{1,0:T(1,128)}, u32[]{:S(2)}) copy-start(f32[1,128]{1,0:T(1,128)} %get-tuple-element.16) | copy-start | bytes 1540

commit v2 on v1

v2 whole, which is shorter than its diff:
```python
import math

import jax
import jax.numpy as jnp
from jax import lax
from jax.experimental import pallas as pl
from jax.experimental.pallas import tpu as pltpu
from jax.sharding import PartitionSpec as P

LOGIT_SCALE = 2.5
STEP_RATE = 0.05
LOG2E = math.log2(math.e)
LN2 = math.log(2.0)
FLOOR = -1e30

BLOCKS = 128
ROWS = 128
WIDTH = 256
ITEMS = 2048
NEGS = 512
STEPS = 64
SLOTS = 256


RING = (0, 1, 3, 2)


def order4(q):
    return jnp.where(q < 2, q, 5 - q)


def head_kernel(
    u_ref, shard_ref, row_ref, negr_ref, lp_ref, table_ref,
    gsum_ref, up_out, r_out, c_out, loss_ref,
    users, scores_own, scores_sib, negs, bias, tab, tabb, ids_all, slot_i, slot_r,
    slot_t, slot_lp, slot_pos, slot_u,
    stat_out, stat_in, norm_all, acc, gsend, grecv, upx, rx, cx,
    block_sem, send_sem, tab_sem, ids_sem, ids_send, stat_sem, stat_send, norm_sem, norm_send,
    pair_send, pair_recv,
):
    me = lax.axis_index("item")
    group = lax.axis_index("batch")
    other = 1 - group
    core = lax.rem(me, 2)
    sib = me + 1 - 2 * core
    x_pos = lax.rem(me // 2, 4)
    z_pos = lax.rem(me // 8, 4)
    y_pos = me // 32
    outer = jnp.where(core == 0, y_pos, x_pos)
    inner = jnp.where(core == 0, x_pos, y_pos)
    s_out = jnp.where(core == 0, 32, 2)
    s_in = 34 - s_out

    def place(do, di, dz):
        return (
            lax.rem(outer + do, 4) * s_out + lax.rem(inner + di, 4) * s_in
            + lax.rem(z_pos + dz, 4) * 8 + core
        )

    def sib_place(do, di, dz):
        return (
            lax.rem(inner + do, 4) * s_in + lax.rem(outer + di, 4) * s_out
            + lax.rem(z_pos + dz, 4) * 8 + 1 - core
        )

    barrier = pltpu.get_barrier_semaphore()
    pl.semaphore_signal(
        barrier, inc=1, device_id={"batch": other}, device_id_type=pl.DeviceIdType.MESH
    )

    @pl.loop(1, BLOCKS)
    def _(j):
        pl.semaphore_signal(
            barrier, inc=1, device_id={"item": lax.rem(me + j, BLOCKS)},
            device_id_type=pl.DeviceIdType.MESH,
        )

    table_copy = pltpu.make_async_copy(table_ref, tab, tab_sem)
    table_copy.start()
    users[me] = u_ref[...]
    ids_all[me] = shard_ref[...] * ITEMS + row_ref[...]
    pl.semaphore_wait(barrier, BLOCKS)

    def block_copy(b, dev):
        return pltpu.make_async_remote_copy(
            src_ref=users.at[b], dst_ref=users.at[b], send_sem=send_sem,
            recv_sem=block_sem.at[b], device_id={"item": dev},
            device_id_type=pl.DeviceIdType.MESH,
        )

    def arrived(b):
        block_copy(b, sib).wait_recv()

    def send(b, *devices):
        for dev in devices:
            block_copy(b, dev).start()

    out_up, out_down = place(1, 0, 0), place(3, 0, 0)
    in_up, in_down = place(0, 1, 0), place(0, 3, 0)
    z_up, z_down = place(0, 0, 1), place(0, 0, 3)

    def forward_plane(q):
        di, dz = RING[q // 4], RING[q % 4]
        b = place(0, di, dz)
        if q > 0:
            arrived(b)
        send(b, out_down, out_up)
        if di == 0:
            send(b, in_down, in_up)
            if dz == 0:
                send(b, z_down, z_up)
            if dz == 3:
                far = place(0, 0, 1 + 2 * core)
                send(far, jnp.where(core == 0, z_down, z_up))
        if di == 1 and q % 2 == 0:
            send(b, in_down)
        if di == 3 and q % 2 == 1:
            send(b, in_up)
        send(b, sib)

    def peer_copy(src, dst, send_to, recv, dev):
        return pltpu.make_async_remote_copy(
            src_ref=src, dst_ref=dst, send_sem=send_to, recv_sem=recv,
            device_id={"item": dev}, device_id_type=pl.DeviceIdType.MESH,
        )

    def wait_bytes(ref, sem):
        pltpu.make_async_copy(ref, ref, sem).wait()

    forward_plane(0)

    @pl.loop(1, BLOCKS)
    def _(j):
        dev = lax.rem(me + j, BLOCKS)
        peer_copy(ids_all.at[me], ids_all.at[me], ids_send, ids_sem, dev).start()

    table_copy.wait()
    tabb[...] = tab[...].astype(jnp.bfloat16)
    lp2 = lp_ref[...] * LOG2E

    def gather(row_cols):
        lane = lax.broadcasted_iota(jnp.int32, row_cols.shape, 1)
        hots = [row_cols == lane + 128 * j for j in range(ITEMS // 128)]
        hot = jnp.concatenate([h.astype(jnp.float32).astype(jnp.bfloat16) for h in hots], axis=1)
        rows = jnp.dot(hot, tabb[...], preferred_element_type=jnp.float32)
        total = jnp.zeros(row_cols.shape, jnp.float32)
        for j, h in enumerate(hots):
            total = total + jnp.where(h, lp2[:, 128 * j : 128 * (j + 1)], 0.0)
        lp_rows = jnp.broadcast_to(jnp.sum(total, axis=1, keepdims=True), row_cols.shape)
        return rows, lp_rows

    neg_cols = jnp.transpose(jnp.broadcast_to(negr_ref[...], (128, NEGS)))
    for q in range(NEGS // 128):
        part = slice(128 * q, 128 * (q + 1))
        rows, lp_rows = gather(neg_cols[part])
        negs[part, :] = rows.astype(jnp.bfloat16)
        bias[part, :] = lp_rows

    for q in range(1, 16):
        forward_plane(q)

    wait_bytes(ids_all.at[pl.ds(0, BLOCKS - 1)], ids_sem)
    ids = ids_all[:, 0, :]
    wide = (BLOCKS, ROWS)
    lane = lax.broadcasted_iota(jnp.int32, wide, 1)
    mine = (ids // ITEMS) == me
    row = lax.rem(ids, ITEMS)
    lo = jnp.broadcast_to(
        jnp.min(jnp.where(mine, lane, ROWS), axis=1, keepdims=True), wide
    )
    hi = jnp.broadcast_to(jnp.max(jnp.where(mine, lane, -1), axis=1, keepdims=True), wide)
    first = mine & (lane == lo)
    last = mine & (lane == hi) & (hi > lo)
    slot_i[0:BLOCKS, :] = jnp.where(lo < ROWS, lo, -1)
    slot_i[BLOCKS:, :] = jnp.where(hi > lo, hi, -1)
    for c, hit in enumerate((first, last)):
        slot_r[BLOCKS * c : BLOCKS * (c + 1), :] = jnp.broadcast_to(
            jnp.max(jnp.where(hit, row, -1), axis=1, keepdims=True), wide
        )
    for q in range(SLOTS // 128):
        part = slice(128 * q, 128 * (q + 1))
        rows, lp_rows = gather(slot_r[part, :])
        slot_t[part, :] = rows
        slot_lp[part, :] = lp_rows

    sub = lax.broadcasted_iota(jnp.int32, (8, 128), 0)
    lane8 = lax.broadcasted_iota(jnp.int32, (8, 128), 1)

    def pick(values):
        out = jnp.broadcast_to(values[3], (8, values[3].shape[1]))
        s8 = lax.broadcasted_iota(jnp.int32, out.shape, 0)
        for c in (2, 1, 0):
            out = jnp.where(s8 == c, values[c], out)
        return out

    def tile_blocks(s):
        near = s - 8
        far = 2 * (s - 24)
        offsets = []
        for h in range(2):
            k = jnp.where(s < 8, 2 * s + h, jnp.where(s < 24, near, far + h))
            do = jnp.where(s < 8, 0, jnp.where(s < 24, 1 + 2 * h, 2))
            offsets.append((do, order4(k // 4), order4(lax.rem(k, 4))))
        return [place(*o) for o in offsets], [sib_place(*o) for o in offsets]

    def both_users(blocks):
        return jnp.concatenate([users[blocks[0]], users[blocks[1]]], axis=0)

    def score(blocks, scores):
        pair = both_users(blocks)
        a, b = blocks
        at = [a, BLOCKS + a, b, BLOCKS + b]
        index = [slot_i[pl.ds(r, 1), :] for r in at]
        left = jnp.where(sub == 0, index[0], jnp.where(sub == 1, index[1], -2)) == lane8
        right = jnp.where(sub == 2, index[2], jnp.where(sub == 3, index[3], -2)) == lane8
        mask = jnp.concatenate([jnp.where(left, 1.0, 0.0), jnp.where(right, 1.0, 0.0)], axis=1)
        hot = jnp.concatenate([mask, jnp.zeros_like(mask)], axis=0).astype(jnp.bfloat16)
        raw = lax.dot_general(
            negs[...], pair, (((1,), (1,)), ((), ())), preferred_element_type=jnp.float32
        )
        cols = bias[...]
        scaled = raw * (LOGIT_SCALE * LOG2E) - jnp.concatenate([cols, cols], axis=1)
        scores[a // 2] = scaled[:, :ROWS]
        scores[b // 2] = scaled[:, ROWS:]
        peak = jnp.max(scaled, axis=0, keepdims=True)
        gathered = jnp.dot(hot, pair, preferred_element_type=jnp.float32)[0:8]
        dots = jnp.sum(
            gathered * pick([slot_t[pl.ds(r, 1), :] for r in at]), axis=1, keepdims=True
        )
        pos = dots * (LOGIT_SCALE * LOG2E) - pick([slot_lp[pl.ds(r, 1), :] for r in at])
        for c, r in enumerate(at):
            slot_u[pl.ds(r, 1), :] = gathered[c : c + 1]
            slot_pos[pl.ds(r, 1), :] = pos[c : c + 1]
        pos_row = jnp.max(
            jnp.where(mask > 0.0, jnp.concatenate([pos, pos], axis=1), FLOOR),
            axis=0, keepdims=True,
        )
        return peak, pos_row

    def summed(blocks, scores, peak, pos_row):
        for h, b in enumerate(blocks):
            part = slice(ROWS * h, ROWS * (h + 1))
            total = jnp.sum(jnp.exp2(scores[b // 2] - peak[:, part]), axis=0, keepdims=True)
            lse = peak[:, part] + jnp.log(total) * LOG2E
            stat_out[b] = jnp.concatenate([lse, pos_row[:, part]], axis=0)

    def tile(s):
        own, sibs = tile_blocks(s)
        first_own = score(own, scores_own)
        first_sib = score(sibs, scores_sib)
        summed(own, scores_own, *first_own)
        summed(sibs, scores_sib, *first_sib)

    def send_stats(b):
        peer_copy(stat_out.at[b], stat_in.at[me], stat_send, stat_sem, b).start()

    def before_tile(s):
        @pl.when(s > 0)
        def _():
            own, sibs = tile_blocks(s - 1)

            @pl.when(s > 1)
            def _():
                send_stats(own[0])

            send_stats(own[1])
            send_stats(sibs[0])
            send_stats(sibs[1])

        for b in tile_blocks(s)[1]:
            arrived(b)

    @pl.loop(0, 8)
    def _(r):
        for h in range(2):
            k = 2 * r + h
            di, dz = order4(k // 4), order4(lax.rem(k, 4))
            b = place(1, di, dz)
            arrived(b)
            if h == 0:
                send(b, out_down)
            send(b, sib)
            b = place(3, di, dz)
            arrived(b)
            if h == 1:
                send(b, out_up)
            send(b, sib)
            before_tile(k)
            tile(k)

    @pl.loop(0, 8)
    def _(r):
        for h in range(2):
            k = 2 * r + h
            b = place(2, order4(k // 4), order4(lax.rem(k, 4)))
            arrived(b)
            send(b, sib)
        for h in range(2):
            before_tile(16 + 2 * r + h)
            tile(16 + 2 * r + h)

    own, sibs = tile_blocks(STEPS // 2 - 1)
    for b in own + sibs:
        send_stats(b)
    stat_in[me] = stat_out[me]

    def pair_copy(src, dst, k):
        return pltpu.make_async_remote_copy(
            src_ref=src, dst_ref=dst, send_sem=pair_send.at[k], recv_sem=pair_recv.at[k],
            device_id={"batch": other}, device_id_type=pl.DeviceIdType.MESH,
        )

    def to_lanes(cols):
        return jnp.concatenate(
            [jnp.transpose(cols[BLOCKS * c : BLOCKS * (c + 1)])[0:8, :] for c in range(2)], axis=1
        )

    wait_bytes(stat_in.at[pl.ds(0, BLOCKS - 1)], stat_sem)
    lses = stat_in[:, 0, :]
    pos_own = jnp.max(stat_in[:, 1, :], axis=0, keepdims=True)
    top = jnp.maximum(jnp.max(lses, axis=0, keepdims=True), pos_own)
    total = jnp.sum(jnp.exp2(lses - top), axis=0, keepdims=True) + jnp.exp2(pos_own - top)
    norm = top + jnp.log(total) * LOG2E
    norm_all[me] = norm

    @pl.loop(1, BLOCKS)
    def _(j):
        dev = lax.rem(me + j, BLOCKS)
        peer_copy(norm_all.at[me], norm_all.at[me], norm_send, norm_sem, dev).start()

    loss_ref[...] = (norm - pos_own) * LN2
    upx[group] = slot_u[...].astype(jnp.bfloat16)
    rx[group] = to_lanes(slot_r[...])
    up_copy = pair_copy(upx.at[group], upx.at[group], 0)
    r_copy = pair_copy(rx.at[group], rx.at[group], 1)
    up_copy.start()
    r_copy.start()
    wait_bytes(norm_all.at[pl.ds(0, BLOCKS - 1)], norm_sem)

    norms = norm_all[:, 0, :]
    lane = lax.broadcasted_iota(jnp.int32, wide, 1)
    coefs = []
    for c in range(2):
        part = slice(BLOCKS * c, BLOCKS * (c + 1))
        index = slot_i[part, :]
        found = jnp.sum(jnp.where(index == lane, norms, 0.0), axis=1, keepdims=True)
        coefficient = jnp.exp2(slot_pos[part, :] - found) - 1.0
        coefs.append(jnp.where(index >= 0, LOGIT_SCALE * coefficient, 0.0))
    cx[group] = to_lanes(jnp.concatenate(coefs, axis=0))
    c_copy = pair_copy(cx.at[group], cx.at[group], 2)
    c_copy.start()

    copies = [up_copy, r_copy, c_copy]
    half = NEGS // 2
    for h in range(2):
        part = slice(half * h, half * (h + 1))
        acc[...] = jnp.zeros_like(acc)

        @pl.loop(0, STEPS // 8)
        def _(g):
            probs, rows = [], []
            for u in range(8):
                c = 8 * g + u
                for scores, b in ((scores_own, 2 * c + core), (scores_sib, 2 * c + 1 - core)):
                    probs.append(
                        jnp.exp2(scores[c, part, :] - norm_all[b]).astype(jnp.bfloat16)
                    )
                    rows.append(users[b])
            acc[...] += jnp.dot(
                jnp.concatenate(probs, axis=1), jnp.concatenate(rows, axis=0),
                preferred_element_type=jnp.float32,
            )

        gsend[h] = acc[...].astype(gsend.dtype)
        g_copy = pair_copy(gsend.at[h], grecv.at[h], 3 + h)
        g_copy.start()
        copies.append(g_copy)

    for copy in copies:
        copy.wait()
    for h in range(2):
        part = slice(half * h, half * (h + 1))
        gsum_ref[part, :] = gsend[h].astype(jnp.float32) + grecv[h].astype(jnp.float32)
    for k in range(2):
        up_out[SLOTS * k : SLOTS * (k + 1), :] = upx[k]
        r_out[:, SLOTS * k : SLOTS * (k + 1)] = rx[k]
        c_out[:, SLOTS * k : SLOTS * (k + 1)] = cx[k]
    wait_bytes(users.at[pl.ds(0, BLOCKS - 1)], send_sem)
    wait_bytes(ids_all.at[pl.ds(0, BLOCKS - 1)], ids_send)
    wait_bytes(stat_in.at[pl.ds(0, BLOCKS - 1)], stat_send)
    wait_bytes(norm_all.at[pl.ds(0, BLOCKS - 1)], norm_send)


def head(u, shards, rows, negr, lp, table):
    f32, bf16, i32 = jnp.float32, jnp.bfloat16, jnp.int32
    vmem = pl.BlockSpec(memory_space=pltpu.VMEM)
    dma = pltpu.SemaphoreType.DMA
    V = pltpu.VMEM
    return pl.pallas_call(
        head_kernel,
        out_shape=(
            jax.ShapeDtypeStruct((NEGS, WIDTH), f32),
            jax.ShapeDtypeStruct((2 * SLOTS, WIDTH), bf16),
            jax.ShapeDtypeStruct((8, 2 * SLOTS), i32),
            jax.ShapeDtypeStruct((8, 2 * SLOTS), f32),
            jax.ShapeDtypeStruct((1, ROWS), f32),
        ),
        in_specs=[vmem] * 5 + [pl.BlockSpec(memory_space=pl.ANY)],
        out_specs=(vmem,) * 5,
        scratch_shapes=[
            V((BLOCKS, ROWS, WIDTH), bf16),
            V((STEPS, NEGS, ROWS), f32),
            V((STEPS, NEGS, ROWS), f32),
            V((NEGS, WIDTH), bf16),
            V((NEGS, 128), f32),
            V((ITEMS, WIDTH), f32),
            V((ITEMS, WIDTH), bf16),
            V((BLOCKS, 1, ROWS), i32),
            V((SLOTS, 128), i32),
            V((SLOTS, 128), i32),
            V((SLOTS, WIDTH), f32),
            V((SLOTS, 128), f32),
            V((SLOTS, 128), f32),
            V((SLOTS, WIDTH), f32),
            V((BLOCKS, 2, ROWS), f32),
            V((BLOCKS, 2, ROWS), f32),
            V((BLOCKS, 1, ROWS), f32),
            V((NEGS // 2, WIDTH), f32),
            V((2, NEGS // 2, WIDTH), bf16),
            V((2, NEGS // 2, WIDTH), bf16),
            V((2, SLOTS, WIDTH), bf16),
            V((2, 8, SLOTS), i32),
            V((2, 8, SLOTS), f32),
            dma((BLOCKS,)),
            dma, dma, dma, dma, dma, dma, dma, dma,
            dma((5,)),
            dma((5,)),
        ],
        compiler_params=pltpu.CompilerParams(
            has_side_effects=True, vmem_limit_bytes=58 * 1024 * 1024, collective_id=0
        ),
        cost_estimate=pl.CostEstimate(
            flops=3 * 2 * 16384 * NEGS * WIDTH, bytes_accessed=4 << 20,
            transcendentals=2 * 16384 * NEGS,
        ),
        name="sampled_head",
    )(u, shards, rows, negr, lp, table)


TILE = 512


def update_kernel(
    negr_ref, r_ref, c_ref, gsum_ref, up_ref, table_ref, accum_ref,
    new_table_ref, new_accum_ref, g_hi, g_lo,
):
    @pl.when(pl.program_id(0) == 0)
    def _():
        g = LOGIT_SCALE * gsum_ref[...]
        top = g.astype(jnp.bfloat16)
        g_hi[...] = top
        g_lo[...] = (g - top.astype(jnp.float32)).astype(jnp.bfloat16)

    row = lax.broadcasted_iota(jnp.int32, (TILE, NEGS), 0) + TILE * pl.program_id(0)
    hot = jnp.where(row == negr_ref[...], 1.0, 0.0).astype(jnp.bfloat16)
    weight = jnp.where(row == r_ref[0:1, :], c_ref[0:1, :], 0.0)
    w_hi = weight.astype(jnp.bfloat16)
    w_lo = (weight - w_hi.astype(jnp.float32)).astype(jnp.bfloat16)

    def mm(a, b):
        return jnp.dot(a, b, preferred_element_type=jnp.float32)

    grad = (mm(hot, g_hi[...]) + mm(hot, g_lo[...])) + (
        mm(w_hi, up_ref[...]) + mm(w_lo, up_ref[...])
    )
    accum = accum_ref[...] + grad * grad
    new_accum_ref[...] = accum
    new_table_ref[...] = table_ref[...] - STEP_RATE * grad * lax.rsqrt(accum)


def update(negr, rows, coefs, gsum, ups, table, accum):
    whole = lambda shape: pl.BlockSpec(shape, lambda i: (0, 0))
    tile = pl.BlockSpec((TILE, WIDTH), lambda i: (i, 0))
    return pl.pallas_call(
        update_kernel,
        grid=(ITEMS // TILE,),
        out_shape=(jax.ShapeDtypeStruct((ITEMS, WIDTH), jnp.float32),) * 2,
        in_specs=[
            whole((1, NEGS)), whole((8, 2 * SLOTS)), whole((8, 2 * SLOTS)),
            whole((NEGS, WIDTH)), whole((2 * SLOTS, WIDTH)), tile, tile,
        ],
        out_specs=(tile, tile),
        scratch_shapes=[pltpu.VMEM((NEGS, WIDTH), jnp.bfloat16)] * 2,
        compiler_params=pltpu.CompilerParams(vmem_limit_bytes=60 * 1024 * 1024),
        name="table_update",
    )(negr, rows, coefs, gsum, ups, table, accum)


def per_device(
    user_vectors, item_table, grad_accum, log_prob, positive_shard, positive_row, negatives
):
    negr = negatives.reshape(1, NEGS)
    gsum, ups, rows, coefs, loss = head(
        user_vectors, positive_shard.reshape(1, ROWS), positive_row.reshape(1, ROWS), negr,
        log_prob.reshape(1, ITEMS), item_table,
    )
    new_table, new_accum = update(negr, rows, coefs, gsum, ups, item_table, grad_accum)
    return (new_table, new_accum, loss.reshape(ROWS))


def solution(mesh):
    in_specs = (
        P(("item", "batch"), None),
        P("item", None),
        P("item", None),
        P("item"),
        P(("item", "batch"), None),
        P(("item", "batch")),
        P("item"),
    )
    out_specs = (P("item", None), P("item", None), P(("item", "batch")))
    return jax.shard_map(
        per_device, mesh=mesh, in_specs=in_specs, out_specs=out_specs, check_vma=False
    )
```

time: 122 us -> 94 us (0.77)
  Pallas kernels: 115 us -> 92.7 us
  local copies, waits for them, and re-layouts: 3.94 us -> 0.52 us
    pallas_call x1, Pallas kernels: 110 us -> 86.2 us  [head(): pl.pallas_call(head_kernel, out_shape=(jax.ShapeDtypeStruct((NEGS, WIDTH)...]
    unnamed x17 -> x3, local copies, waits for them, and re-layouts: 3.94 us -> 0.52 us
where the time goes in v2:
time: 94 us; the launch traced here: 93.8 us
  Pallas kernels  92.7 us (99%)
    pallas_call x1, Pallas kernels, head(): pl.pallas_call(head_kernel, out_shape=(jax.ShapeDtypeStruct((NEGS, WIDTH)...  86.2 us
    pallas_call x1, Pallas kernels, update(): pl.pallas_call(update_kernel, grid=(ITEMS // TILE,), out_shape=(jax.Shape...  6.49 us

profile of v2, /device:TPU:1, one launch (start us, length us, event | category | flops | bytes accessed | tf_op | source)
XLA Modules:
  0.0 93.8 jit_solution(10565856877401635787)
XLA Ops:
  0.6 86.2 %sampled_head.1 = (f32[512,256]{1,0:T(8,128)}, bf16[512,256]{1,0:T(8,128)(2,1)}, s32[8,512]{1,0:T(8,128)}, f32[8,512]{1,0:T(8,128)}, f32[1,128]{1,0:T(1,128)}) custom-call(bf16[128,256]{1,0:T(8,128)(2,1)} %u_ref.1, s32[1,128]{1,0:T(1,128)} %bitcast.8, s32[1,128]{1,0:T(1,128)} %bitcast.9, s32[1,512]{1,0:T(1,128)} %bitcast.5, f32[1,2048]{1,0:T(1,128)} %bitcast.7, ...), custom_call_target="tpu_custom_call" | custom-call | flops 12884901888 | bytes 4194304 | tf_op jit(solution)/shard_map/sampled_head/pallas_call | solution.py:399
  86.8 0.0 copy-start
  86.8 6.5 %table_update.1 = (f32[2048,256]{1,0:T(8,128)}, f32[2048,256]{1,0:T(8,128)}) custom-call(s32[1,512]{1,0:T(1,128)} %bitcast.6, s32[8,512]{1,0:T(8,128)} %get-tuple-element.10.r_ref, f32[8,512]{1,0:T(8,128)} %get-tuple-element.11.c_ref, f32[512,256]{1,0:T(8,128)} %get-tuple-element.12.gsum_ref, bf16[512,256]{1,0:T(8,128)(2,1)} %get-tuple-element.13.up_ref, ...), custom_call_target="tpu_custom_call" | custom-call | tf_op jit(solution)/shard_map/table_update/pallas_call | solution.py:484
  93.3 0.0 copy-done
  93.3 0.5 copy.11
Async XLA Ops:
  86.8 6.5 %copy-start = (f32[1,128]{1,0:T(1,128)S(1)}, f32[1,128]{1,0:T(1,128)}, u32[]{:S(2)}) copy-start(f32[1,128]{1,0:T(1,128)} %get-tuple-element.16) | copy-start | bytes 1540

commit v3 on v2

--- a/solution.py
+++ b/solution.py
@@ -19,6 +19,7 @@
 ITEMS = 2048
 NEGS = 512
 STEPS = 64
+AHEAD = 1
 SLOTS = 256
 
 
@@ -99,23 +100,32 @@
     in_up, in_down = place(0, 1, 0), place(0, 3, 0)
     z_up, z_down = place(0, 0, 1), place(0, 0, 3)
 
-    def forward_plane(q):
-        di, dz = RING[q // 4], RING[q % 4]
-        b = place(0, di, dz)
-        if q > 0:
+    def plane_block(ki, j):
+        dz = RING[j]
+        b = place(0, order4(ki), dz)
+        if j == 0:
+
+            @pl.when(ki > 0)
+            def _():
+                arrived(b)
+        else:
             arrived(b)
-        send(b, out_down, out_up)
-        if di == 0:
-            send(b, in_down, in_up)
-            if dz == 0:
+
+        @pl.when(ki == 0)
+        def _():
+            if j == 0:
                 send(b, z_down, z_up)
-            if dz == 3:
+            if j == 2:
                 far = place(0, 0, 1 + 2 * core)
                 send(far, jnp.where(core == 0, z_down, z_up))
-        if di == 1 and q % 2 == 0:
-            send(b, in_down)
-        if di == 3 and q % 2 == 1:
-            send(b, in_up)
+            send(b, in_down, in_up)
+
+        send(b, out_down, out_up)
+
+        @pl.when(ki == (1 if j % 2 == 0 else 2))
+        def _():
+            send(b, in_down if j % 2 == 0 else in_up)
+
         send(b, sib)
 
     def peer_copy(src, dst, send_to, recv, dev):
@@ -127,7 +137,7 @@
     def wait_bytes(ref, sem):
         pltpu.make_async_copy(ref, ref, sem).wait()
 
-    forward_plane(0)
+    plane_block(jnp.int32(0), 0)
 
     @pl.loop(1, BLOCKS)
     def _(j):
@@ -156,8 +166,8 @@
         negs[part, :] = rows.astype(jnp.bfloat16)
         bias[part, :] = lp_rows
 
-    for q in range(1, 16):
-        forward_plane(q)
+    for q in range(1, 4 * AHEAD):
+        plane_block(jnp.int32(q // 4), q % 4)
 
     wait_bytes(ids_all.at[pl.ds(0, BLOCKS - 1)], ids_sem)
     ids = ids_all[:, 0, :]
@@ -244,64 +254,72 @@
             lse = peak[:, part] + jnp.log(total) * LOG2E
             stat_out[b] = jnp.concatenate([lse, pos_row[:, part]], axis=0)
 
+    def send_stats(b):
+        peer_copy(stat_out.at[b], stat_in.at[me], stat_send, stat_sem, b).start()
+
     def tile(s):
         own, sibs = tile_blocks(s)
+        for b in sibs:
+            arrived(b)
         first_own = score(own, scores_own)
         first_sib = score(sibs, scores_sib)
         summed(own, scores_own, *first_own)
         summed(sibs, scores_sib, *first_sib)
 
-    def send_stats(b):
-        peer_copy(stat_out.at[b], stat_in.at[me], stat_send, stat_sem, b).start()
-
-    def before_tile(s):
         @pl.when(s > 0)
         def _():
-            own, sibs = tile_blocks(s - 1)
-
-            @pl.when(s > 1)
+            send_stats(own[0])
+
+        send_stats(own[1])
+        send_stats(sibs[0])
+        send_stats(sibs[1])
+
+    def far_block(ki, j):
+        b = place(2, order4(ki), RING[j])
+        arrived(b)
+        send(b, sib)
+
+    @pl.loop(0, 4)
+    def _(m):
+        for j in range(4):
+
+            @pl.when(m < 4 - AHEAD)
             def _():
-                send_stats(own[0])
-
-            send_stats(own[1])
-            send_stats(sibs[0])
-            send_stats(sibs[1])
-
-        for b in tile_blocks(s)[1]:
-            arrived(b)
-
-    @pl.loop(0, 8)
-    def _(r):
-        for h in range(2):
-            k = 2 * r + h
-            di, dz = order4(k // 4), order4(lax.rem(k, 4))
-            b = place(1, di, dz)
-            arrived(b)
-            if h == 0:
-                send(b, out_down)
-            send(b, sib)
-            b = place(3, di, dz)
-            arrived(b)
-            if h == 1:
-                send(b, out_up)
-            send(b, sib)
-            before_tile(k)
-            tile(k)
-
-    @pl.loop(0, 8)
-    def _(r):
-        for h in range(2):
-            k = 2 * r + h
-            b = place(2, order4(k // 4), order4(lax.rem(k, 4)))
-            arrived(b)
-            send(b, sib)
-        for h in range(2):
-            before_tile(16 + 2 * r + h)
-            tile(16 + 2 * r + h)
-
-    own, sibs = tile_blocks(STEPS // 2 - 1)
-    for b in own + sibs:
-        send_stats(b)
+                plane_block(m + AHEAD, j)
+
+            di, dz = order4(m), RING[j]
+            b1, b3 = place(1, di, dz), place(3, di, dz)
+            arrived(b1)
+            if j % 2 == 0:
+                send(b1, out_down)
+            send(b1, sib)
+            arrived(b3)
+            if j % 2 == 1:
+                send(b3, out_up)
+            send(b3, sib)
+
+            @pl.when(m > 0)
+            def _():
+                far_block(m - 1, j)
+
+            k = 4 * m + j
+            rest = 24 + (k - 6) // 2 if j % 2 == 0 else (k - 1) // 2
+
+            @pl.loop(0, 2)
+            def _(e):
+                s = jnp.where(e == 0, k + 6, rest)
+
+                @pl.when(k >= jnp.where(e == 0, 2, 6 if j % 2 == 0 else 0))
+                def _():
+                    tile(s)
+
+    for j in range(4):
+        far_block(3, j)
+
+    @pl.loop(0, 5)
+    def _(e):
+        tile(jnp.where(e < 2, 22 + e, 27 + e))
+
     stat_in[me] = stat_out[me]
 
     def pair_copy(src, dst, k):

time: 94 us -> 88.1 us (0.937)
  Pallas kernels: 92.7 us -> 86.7 us
    pallas_call x1, Pallas kernels: 86.2 us -> 80.2 us  [head(): pl.pallas_call(head_kernel, out_shape=(jax.ShapeDtypeStruct((NEGS, WIDTH)...]
where the time goes in v3:
time: 88.1 us; the launch traced here: 87.9 us
  Pallas kernels  86.7 us (98%)
    pallas_call x1, Pallas kernels, head(): pl.pallas_call(head_kernel, out_shape=(jax.ShapeDtypeStruct((NEGS, WIDTH)...  80.2 us
    pallas_call x1, Pallas kernels, update(): pl.pallas_call(update_kernel, grid=(ITEMS // TILE,), out_shape=(jax.Shape...  6.49 us

profile of v3, /device:TPU:1, one launch (start us, length us, event | category | flops | bytes accessed | tf_op | source)
XLA Modules:
  0.0 87.9 jit_solution(3208952762298204284)
XLA Ops:
  0.6 80.2 %sampled_head.1 = (f32[512,256]{1,0:T(8,128)}, bf16[512,256]{1,0:T(8,128)(2,1)}, s32[8,512]{1,0:T(8,128)}, f32[8,512]{1,0:T(8,128)}, f32[1,128]{1,0:T(1,128)}) custom-call(bf16[128,256]{1,0:T(8,128)(2,1)} %u_ref.1, s32[1,128]{1,0:T(1,128)} %bitcast.8, s32[1,128]{1,0:T(1,128)} %bitcast.9, s32[1,512]{1,0:T(1,128)} %bitcast.5, f32[1,2048]{1,0:T(1,128)} %bitcast.7, ...), custom_call_target="tpu_custom_call" | custom-call | flops 12884901888 | bytes 4194304 | tf_op jit(solution)/shard_map/sampled_head/pallas_call | solution.py:417
  80.9 0.0 copy-start
  80.9 6.5 %table_update.1 = (f32[2048,256]{1,0:T(8,128)}, f32[2048,256]{1,0:T(8,128)}) custom-call(s32[1,512]{1,0:T(1,128)} %bitcast.6, s32[8,512]{1,0:T(8,128)} %get-tuple-element.10.r_ref, f32[8,512]{1,0:T(8,128)} %get-tuple-element.11.c_ref, f32[512,256]{1,0:T(8,128)} %get-tuple-element.12.gsum_ref, bf16[512,256]{1,0:T(8,128)(2,1)} %get-tuple-element.13.up_ref, ...), custom_call_target="tpu_custom_call" | custom-call | tf_op jit(solution)/shard_map/table_update/pallas_call | solution.py:502
  87.4 0.0 copy-done
  87.4 0.5 copy.11
Async XLA Ops:
  80.9 6.5 %copy-start = (f32[1,128]{1,0:T(1,128)S(1)}, f32[1,128]{1,0:T(1,128)}, u32[]{:S(2)}) copy-start(f32[1,128]{1,0:T(1,128)} %get-tuple-element.16) | copy-start | bytes 1540

commit v4 on v3

--- a/solution.py
+++ b/solution.py
@@ -69,18 +69,26 @@
         barrier, inc=1, device_id={"batch": other}, device_id_type=pl.DeviceIdType.MESH
     )
 
-    @pl.loop(1, BLOCKS)
+    def greet(dev):
+        pl.semaphore_signal(
+            barrier, inc=1, device_id={"item": dev}, device_id_type=pl.DeviceIdType.MESH
+        )
+
+    row_start = (me // 8) * 8
+
+    @pl.loop(1, 8)
     def _(j):
-        pl.semaphore_signal(
-            barrier, inc=1, device_id={"item": lax.rem(me + j, BLOCKS)},
-            device_id_type=pl.DeviceIdType.MESH,
-        )
+        greet(row_start + lax.rem(me + j, 8))
+
+    @pl.loop(1, 16)
+    def _(j):
+        greet(lax.rem(me + 8 * j, BLOCKS))
 
     table_copy = pltpu.make_async_copy(table_ref, tab, tab_sem)
     table_copy.start()
     users[me] = u_ref[...]
     ids_all[me] = shard_ref[...] * ITEMS + row_ref[...]
-    pl.semaphore_wait(barrier, BLOCKS)
+    pl.semaphore_wait(barrier, 23)
 
     def block_copy(b, dev):
         return pltpu.make_async_remote_copy(
@@ -139,10 +147,10 @@
 
     plane_block(jnp.int32(0), 0)
 
-    @pl.loop(1, BLOCKS)
+    @pl.loop(1, 8)
     def _(j):
-        dev = lax.rem(me + j, BLOCKS)
-        peer_copy(ids_all.at[me], ids_all.at[me], ids_send, ids_sem, dev).start()
+        dev = row_start + lax.rem(me + j, 8)
+        peer_copy(ids_all.at[me], ids_all.at[me], ids_send.at[0], ids_sem.at[0], dev).start()
 
     table_copy.wait()
     tabb[...] = tab[...].astype(jnp.bfloat16)
@@ -159,6 +167,14 @@
         lp_rows = jnp.broadcast_to(jnp.sum(total, axis=1, keepdims=True), row_cols.shape)
         return rows, lp_rows
 
+    wait_bytes(ids_all.at[pl.ds(0, 7)], ids_sem.at[0])
+    ids_row = ids_all.at[pl.ds(row_start, 8)]
+
+    @pl.loop(1, 16)
+    def _(j):
+        dev = lax.rem(me + 8 * j, BLOCKS)
+        peer_copy(ids_row, ids_row, ids_send.at[1], ids_sem.at[1], dev).start()
+
     neg_cols = jnp.transpose(jnp.broadcast_to(negr_ref[...], (128, NEGS)))
     for q in range(NEGS // 128):
         part = slice(128 * q, 128 * (q + 1))
@@ -166,10 +182,10 @@
         negs[part, :] = rows.astype(jnp.bfloat16)
         bias[part, :] = lp_rows
 
-    for q in range(1, 4 * AHEAD):
-        plane_block(jnp.int32(q // 4), q % 4)
-
-    wait_bytes(ids_all.at[pl.ds(0, BLOCKS - 1)], ids_sem)
+    plane_block(jnp.int32(0), 1)
+    plane_block(jnp.int32(0), 2)
+
+    wait_bytes(ids_all.at[pl.ds(0, BLOCKS - 8)], ids_sem.at[1])
     ids = ids_all[:, 0, :]
     wide = (BLOCKS, ROWS)
     lane = lax.broadcasted_iota(jnp.int32, wide, 1)
@@ -193,6 +209,9 @@
         slot_t[part, :] = rows
         slot_lp[part, :] = lp_rows
 
+    for q in range(3, 4 * AHEAD):
+        plane_block(jnp.int32(q // 4), q % 4)
+
     sub = lax.broadcasted_iota(jnp.int32, (8, 128), 0)
     lane8 = lax.broadcasted_iota(jnp.int32, (8, 128), 1)
 
@@ -404,7 +423,8 @@
         r_out[:, SLOTS * k : SLOTS * (k + 1)] = rx[k]
         c_out[:, SLOTS * k : SLOTS * (k + 1)] = cx[k]
     wait_bytes(users.at[pl.ds(0, BLOCKS - 1)], send_sem)
-    wait_bytes(ids_all.at[pl.ds(0, BLOCKS - 1)], ids_send)
+    wait_bytes(ids_all.at[pl.ds(0, 7)], ids_send.at[0])
+    wait_bytes(ids_all.at[pl.ds(0, BLOCKS - 8)], ids_send.at[1])
     wait_bytes(stat_in.at[pl.ds(0, BLOCKS - 1)], stat_send)
     wait_bytes(norm_all.at[pl.ds(0, BLOCKS - 1)], norm_send)
 
@@ -450,7 +470,7 @@
             V((2, 8, SLOTS), i32),
             V((2, 8, SLOTS), f32),
             dma((BLOCKS,)),
-            dma, dma, dma, dma, dma, dma, dma, dma,
+            dma, dma, dma((2,)), dma((2,)), dma, dma, dma, dma,
             dma((5,)),
             dma((5,)),
         ],

time: 88.1 us -> 85.5 us (0.970)
  Pallas kernels: 86.7 us -> 84.1 us
    pallas_call x1, Pallas kernels: 80.2 us -> 77.6 us  [head(): pl.pallas_call(head_kernel, out_shape=(jax.ShapeDtypeStruct((NEGS, WIDTH)...]
where the time goes in v4:
time: 85.5 us; the launch traced here: 85.2 us
  Pallas kernels  84.1 us (98%)
    pallas_call x1, Pallas kernels, head(): pl.pallas_call(head_kernel, out_shape=(jax.ShapeDtypeStruct((NEGS, WIDTH)...  77.6 us
    pallas_call x1, Pallas kernels, update(): pl.pallas_call(update_kernel, grid=(ITEMS // TILE,), out_shape=(jax.Shape...  6.49 us

profile of v4, /device:TPU:1, one launch (start us, length us, event | category | flops | bytes accessed | tf_op | source)
XLA Modules:
  0.0 85.2 jit_solution(4919988961828423830)
XLA Ops:
  0.6 77.6 %sampled_head.1 = (f32[512,256]{1,0:T(8,128)}, bf16[512,256]{1,0:T(8,128)(2,1)}, s32[8,512]{1,0:T(8,128)}, f32[8,512]{1,0:T(8,128)}, f32[1,128]{1,0:T(1,128)}) custom-call(bf16[128,256]{1,0:T(8,128)(2,1)} %u_ref.1, s32[1,128]{1,0:T(1,128)} %bitcast.8, s32[1,128]{1,0:T(1,128)} %bitcast.9, s32[1,512]{1,0:T(1,128)} %bitcast.5, f32[1,2048]{1,0:T(1,128)} %bitcast.7, ...), custom_call_target="tpu_custom_call" | custom-call | flops 12884901888 | bytes 4194304 | tf_op jit(solution)/shard_map/sampled_head/pallas_call | solution.py:437
  78.2 0.0 copy-start
  78.2 6.5 %table_update.1 = (f32[2048,256]{1,0:T(8,128)}, f32[2048,256]{1,0:T(8,128)}) custom-call(s32[1,512]{1,0:T(1,128)} %bitcast.6, s32[8,512]{1,0:T(8,128)} %get-tuple-element.10.r_ref, f32[8,512]{1,0:T(8,128)} %get-tuple-element.11.c_ref, f32[512,256]{1,0:T(8,128)} %get-tuple-element.12.gsum_ref, bf16[512,256]{1,0:T(8,128)(2,1)} %get-tuple-element.13.up_ref, ...), custom_call_target="tpu_custom_call" | custom-call | tf_op jit(solution)/shard_map/table_update/pallas_call | solution.py:522
  84.7 0.0 copy-done
  84.7 0.5 copy.11
Async XLA Ops:
  78.2 6.5 %copy-start = (f32[1,128]{1,0:T(1,128)S(1)}, f32[1,128]{1,0:T(1,128)}, u32[]{:S(2)}) copy-start(f32[1,128]{1,0:T(1,128)} %get-tuple-element.16) | copy-start | bytes 1540

commit v5 on v4

--- a/solution.py
+++ b/solution.py
@@ -276,22 +276,26 @@
     def send_stats(b):
         peer_copy(stat_out.at[b], stat_in.at[me], stat_send, stat_sem, b).start()
 
-    def tile(s):
-        own, sibs = tile_blocks(s)
-        for b in sibs:
-            arrived(b)
-        first_own = score(own, scores_own)
-        first_sib = score(sibs, scores_sib)
-        summed(own, scores_own, *first_own)
-        summed(sibs, scores_sib, *first_sib)
-
-        @pl.when(s > 0)
-        def _():
-            send_stats(own[0])
-
-        send_stats(own[1])
-        send_stats(sibs[0])
-        send_stats(sibs[1])
+    def tiles(*several):
+        found = [tile_blocks(s) for s in several]
+        for _, sibs in found:
+            for b in sibs:
+                arrived(b)
+        halves = []
+        for own, sibs in found:
+            halves.append((own, scores_own, score(own, scores_own)))
+            halves.append((sibs, scores_sib, score(sibs, scores_sib)))
+        for blocks, scores, made in halves:
+            summed(blocks, scores, *made)
+        for s, (own, sibs) in zip(several, found):
+
+            @pl.when(s > 0)
+            def _():
+                send_stats(own[0])
+
+            send_stats(own[1])
+            send_stats(sibs[0])
+            send_stats(sibs[1])
 
     def far_block(ki, j):
         b = place(2, order4(ki), RING[j])
@@ -324,20 +328,26 @@
             k = 4 * m + j
             rest = 24 + (k - 6) // 2 if j % 2 == 0 else (k - 1) // 2
 
-            @pl.loop(0, 2)
-            def _(e):
-                s = jnp.where(e == 0, k + 6, rest)
-
-                @pl.when(k >= jnp.where(e == 0, 2, 6 if j % 2 == 0 else 0))
+            least = (6, 3, 6, 3)[j]
+
+            @pl.when(k >= least)
+            def _():
+                tiles(k + 6, rest)
+
+            if j < 3:
+
+                @pl.when((k > 0) & (k < least))
                 def _():
-                    tile(s)
+                    tiles(rest if j == 1 else k + 6)
 
     for j in range(4):
         far_block(3, j)
 
-    @pl.loop(0, 5)
+    @pl.loop(0, 2)
     def _(e):
-        tile(jnp.where(e < 2, 22 + e, 27 + e))
+        tiles(22 + 7 * e, 23 + 7 * e)
+
+    tiles(jnp.int32(31))
 
     stat_in[me] = stat_out[me]
 

time: 85.5 us -> 83.6 us (0.978)
  Pallas kernels: 84.1 us -> 82.2 us
    pallas_call x1, Pallas kernels: 77.6 us -> 75.7 us  [head(): pl.pallas_call(head_kernel, out_shape=(jax.ShapeDtypeStruct((NEGS, WIDTH)...]
where the time goes in v5:
time: 83.6 us; the launch traced here: 83.4 us
  Pallas kernels  82.2 us (98%)
    pallas_call x1, Pallas kernels, head(): pl.pallas_call(head_kernel, out_shape=(jax.ShapeDtypeStruct((NEGS, WIDTH)...  75.7 us
    pallas_call x1, Pallas kernels, update(): pl.pallas_call(update_kernel, grid=(ITEMS // TILE,), out_shape=(jax.Shape...  6.49 us

profile of v5, /device:TPU:1, one launch (start us, length us, event | category | flops | bytes accessed | tf_op | source)
XLA Modules:
  0.0 83.4 jit_solution(13534357023838652775)
XLA Ops:
  0.6 75.7 %sampled_head.1 = (f32[512,256]{1,0:T(8,128)}, bf16[512,256]{1,0:T(8,128)(2,1)}, s32[8,512]{1,0:T(8,128)}, f32[8,512]{1,0:T(8,128)}, f32[1,128]{1,0:T(1,128)}) custom-call(bf16[128,256]{1,0:T(8,128)(2,1)} %u_ref.1, s32[1,128]{1,0:T(1,128)} %bitcast.8, s32[1,128]{1,0:T(1,128)} %bitcast.9, s32[1,512]{1,0:T(1,128)} %bitcast.5, f32[1,2048]{1,0:T(1,128)} %bitcast.7, ...), custom_call_target="tpu_custom_call" | custom-call | flops 12884901888 | bytes 4194304 | tf_op jit(solution)/shard_map/sampled_head/pallas_call | solution.py:447
  76.3 0.0 copy-start
  76.3 6.5 %table_update.1 = (f32[2048,256]{1,0:T(8,128)}, f32[2048,256]{1,0:T(8,128)}) custom-call(s32[1,512]{1,0:T(1,128)} %bitcast.6, s32[8,512]{1,0:T(8,128)} %get-tuple-element.10.r_ref, f32[8,512]{1,0:T(8,128)} %get-tuple-element.11.c_ref, f32[512,256]{1,0:T(8,128)} %get-tuple-element.12.gsum_ref, bf16[512,256]{1,0:T(8,128)(2,1)} %get-tuple-element.13.up_ref, ...), custom_call_target="tpu_custom_call" | custom-call | tf_op jit(solution)/shard_map/table_update/pallas_call | solution.py:532
  82.8 0.0 copy-done
  82.8 0.5 copy.11
Async XLA Ops:
  76.3 6.5 %copy-start = (f32[1,128]{1,0:T(1,128)S(1)}, f32[1,128]{1,0:T(1,128)}, u32[]{:S(2)}) copy-start(f32[1,128]{1,0:T(1,128)} %get-tuple-element.16) | copy-start | bytes 1540
